TPU v7x, 256 devices: a whole 4x4x8 slice. The times are simulated.
256 devices in a mesh: var: 16 (over z, core), layer: 16 (over y, x).
Axes of the slice: x: 4, y: 4, z: 8, core: 2. Of those that a mesh axis runs over, the one named last changes fastest.
Arguments:
- sample_matrix: bfloat16 [1024, 65536], P('layer', 'var'), may hold values from -6 to 6
- precision_blocks: float32 [256, 256, 4, 256], P('layer', 'var'), may hold values from -1 to 2, as said below
- block_pattern: int32 [256, 4], P('var'), may hold values from 0 to 255, as said below
- block_counts: int32 [256], P('var'), may hold values from 1 to 4
- candidate_cols: int32 [256, 6], P('var'), may hold values from 0 to 255, as said below
Outputs:
- updated_blocks: float32 [256, 256, 6, 256], P('layer', 'var')
Inputs may be any that keep to these rules, and one draw needn't show every extreme that they name: `block_pattern`: slot 0 of block row i is i; the 4 entries of a row are distinct. `candidate_cols`: slot 0 of block row i is i; the 6 entries of a row are distinct and include every entry of that row of block_pattern. `precision_blocks`: entry (r, r) of slot 0 of every block row lies in 0.5 to 2.
All inputs are finite; a program needn't handle non-finite values.
Results may differ from a plain program's by a relative error of at most 0.014.
Values may be sent and summed in bfloat16 or wider, within the bound.
A program may use at most 128 MiB of HBM per device.

v0:
```python
import jax
import jax.numpy as jnp
from jax import lax
from jax.sharding import PartitionSpec as P

step_size = 0.5
penalty = 0.04


def body(sample_matrix, precision_blocks, block_pattern, block_counts, candidate_cols):
    layer_count = lax.axis_size("layer")
    layer_index = lax.axis_index("layer")
    rows_here, local_rows, stored, block_width = precision_blocks.shape
    per_layer = sample_matrix.shape[0]
    chosen_count = candidate_cols.shape[1]
    total_samples = per_layer * layer_count
    live_slots = jnp.arange(stored)[None, :] < block_counts[:, None]
    half_blocks = jnp.where(live_slots[None, :, :, None], precision_blocks, 0.0).astype(
        jnp.bfloat16
    )
    gathered = lax.all_gather(sample_matrix, "var", axis=1, tiled=True)
    column_blocks = gathered.reshape(per_layer, gathered.shape[1] // block_width, block_width)
    needed = jnp.take(column_blocks, block_pattern, axis=1)
    local_products = jnp.einsum(
        "rikc,sikc->isr",
        lax.all_gather(half_blocks, "layer", axis=0, tiled=True),
        needed,
        preferred_element_type=jnp.float32,
    ).astype(jnp.bfloat16)
    all_products = lax.all_gather(local_products, "var", axis=0, tiled=True)
    own_columns = sample_matrix.reshape(per_layer, local_rows, block_width)
    far_columns = jnp.take(column_blocks, candidate_cols, axis=1)
    far_products = jnp.take(all_products, candidate_cols, axis=0)
    left_terms = jnp.einsum(
        "sir,icsq->ricq", own_columns, far_products, preferred_element_type=jnp.float32
    )
    right_terms = jnp.einsum(
        "isr,sicq->ricq", local_products, far_columns, preferred_element_type=jnp.float32
    )
    summed = lax.psum_scatter(
        (left_terms + right_terms).astype(jnp.bfloat16), "layer", scatter_dimension=0, tiled=True
    ).astype(jnp.float32)
    gradient = summed / (2.0 * total_samples)
    global_rows = layer_index * rows_here + jnp.arange(rows_here)
    eye_mask = global_rows[:, None] == jnp.arange(block_width)[None, :]
    diagonal = jnp.sum(jnp.where(eye_mask[:, None, :], precision_blocks[:, :, 0, :], 0.0), axis=2)
    first_slot = jnp.arange(chosen_count) == 0
    diag_mask = eye_mask[:, None, None, :] & first_slot[None, None, :, None]
    gradient = gradient - jnp.where(diag_mask, (1.0 / diagonal)[:, :, None, None], 0.0)
    matches = (candidate_cols[:, :, None] == block_pattern[:, None, :]) & live_slots[:, None, :]
    previous = jnp.zeros(gradient.shape, jnp.float32)
    for slot_index in range(stored):
        previous = previous + jnp.where(
            matches[None, :, :, slot_index, None], precision_blocks[:, :, None, slot_index, :], 0.0
        )
    stepped = previous - step_size * gradient
    shrunk = jnp.sign(stepped) * jnp.maximum(jnp.abs(stepped) - step_size * penalty, 0.0)
    return jnp.where(diag_mask, stepped, shrunk)


def solution(mesh):
    placed = (
        P("layer", "var"),
        P("layer", "var", None, None),
        P("var", None),
        P("var"),
        P("var", None),
    )
    return jax.shard_map(
        body, mesh=mesh, in_specs=placed, out_specs=P("layer", "var", None, None), check_vma=False
    )
```

profile of v0, /device:TPU:1, one launch (start us, length us, event | category | flops | bytes accessed | tf_op | source)
XLA Modules:
  0.0 373.0 jit_solution(11819442280027023284)
XLA Ops:
  6.5 0.7 all-gather.4.cloned.1.call-update
  7.3 0.0 all-gather.6.cloned.1.call-start
  7.3 0.7 iota_compare_fusion.1
  8.0 2.7 fusion.19
  10.7 0.0 all-gather.8.cloned.1.call-start
  10.8 0.1 copy.76
  10.9 0.1 reshape.113
  11.0 0.1 copy.75
  11.1 58.3 %all-gather.4.cloned.1.call-done = bf16[64,65536]{1,0:T(8,128)(2,1)} async-done(((bf16[64,4096]{1,0:T(8,128)(2,1)}), bf16[64,65536]{1,0:T(8,128)(2,1)}) %all-gather.4.cloned.1.call-update) | async-done | bytes 8388624 | tf_op jit(solution)/shard_map/all_gather | solution.py:21
  69.4 7.8 %copy.106 = bf16[8,256,8,256]{3,2,0,1:T(8,128)(2,1)} copy(bf16[8,256,8,256]{3,2,1,0:T(8,128)(2,1)} %bitcast.56) | data formatting | bytes 16777216 | tf_op jit(solution)/shard_map/reshape | solution.py:22
  77.2 4.1 %gather_fusion = bf16[64,64,256]{2,1,0:T(8,128)(2,1)S(1)} fusion(bf16[64,256,256]{2,0,1:T(8,128)(2,1)} %bitcast.53, s32[1024]{0:T(1024)S(1)} %pad_clamp_fusion.1), kind=kCustom, calls=%fused_computation | custom fusion | bytes 4194560 | tf_op jit(solution)/shard_map/jit(_take)/gather | solution.py:23
  81.2 71.2 %all-gather.6.cloned.1.call-done = bf16[256,16,4,256]{3,0,2,1:T(8,128)(2,1)} async-done(((bf16[16,16,4,256]{3,0,2,1:T(8,128)(2,1)}), bf16[256,16,4,256]{3,0,2,1:T(8,128)(2,1)}) %all-gather.6.cloned.1.call-update) | async-done | bytes 8388624 | tf_op jit(solution)/shard_map/all_gather | solution.py:26
  152.5 6.9 %fusion.16 = bf16[16,64,256]{2,1,0:T(8,128)(2,1)} fusion(bf16[256,16,4,256]{3,0,2,1:T(8,128)(2,1)} %all-gather.6.cloned.1.call-done, bf16[16,4,64,256]{3,2,1,0:T(8,128)(2,1)S(1)} %bitcast.57, pred[16,4]{1,0:T(8,128)(4,1)S(1)} %copy.75), kind=kOutput, calls=%fused_computation.20 | convolution fusion | flops 538181632 | bytes 11010112 | tf_op jit(solution)/shard_map/rikc,sikc->isr/dot_general | solution.py:24
  159.4 0.0 reduce-scatter.2.cloned.1.call-start
  159.4 0.1 copy.79
  159.5 0.1 reshape.121
  159.6 0.1 copy.74
  159.7 0.9 copy.93
  160.7 5.9 %gather_fusion.2 = bf16[96,64,256]{2,1,0:T(8,128)(2,1)} fusion(bf16[64,256,256]{2,0,1:T(8,128)(2,1)} %bitcast.54, s32[1024]{0:T(1024)S(1)} %pad_clamp_fusion), kind=kCustom, calls=%fused_computation.2 | custom fusion | bytes 6291840 | tf_op jit(solution)/shard_map/jit(_take)/gather | solution.py:32
  166.5 49.6 %all-gather.8.cloned.1.call-done = bf16[256,64,256]{2,1,0:T(8,128)(2,1)} async-done(((bf16[16,64,256]{2,1,0:T(8,128)(2,1)}), bf16[256,64,256]{2,1,0:T(8,128)(2,1)}) %all-gather.8.cloned.1.call-update) | async-done | bytes 8388624 | tf_op jit(solution)/shard_map/all_gather | solution.py:30
  216.2 4.2 %gather_fusion.1 = bf16[96,64,256]{2,1,0:T(8,128)(2,1)S(1)} fusion(bf16[256,64,256]{2,1,0:T(8,128)(2,1)} %all-gather.8.cloned.1.call-done, s32[1024]{0:T(1024)S(1)} %pad_clamp_fusion), kind=kCustom, calls=%fused_computation.1 | custom fusion | bytes 6291840 | tf_op jit(solution)/shard_map/jit(_take)/gather | solution.py:33
  220.3 12.7 %fusion.3 = f32[16,6,256,256]{3,2,1,0:T(8,128)} fusion(bf16[16,6,64,256]{3,2,1,0:T(8,128)(2,1)S(1)} %bitcast.52, pred[16,6]{1,0:T(8,128)(4,1)S(1)} %copy.74, bf16[64,16,256,1]{2,1,0,3:T(8,128)(2,1)} %bitcast.58), kind=kOutput, calls=%fused_computation.8 | convolution fusion | flops 806879232 | bytes 28835936 | tf_op jit(solution)/shard_map/sir,icsq->ricq/dot_general | solution.py:34
  233.1 15.3 %fusion = bf16[256,16,6,256]{0,3,2,1:T(8,128)(2,1)} fusion(f32[16,6,256,256]{3,2,1,0:T(8,128)} %fusion.3, bf16[16,6,64,256]{3,2,1,0:T(8,128)(2,1)} %bitcast.55, pred[16,6]{1,0:T(8,128)(4,1)S(1)} %copy.74, bf16[16,64,256]{2,1,0:T(8,128)(2,1)} %fusion.16), kind=kOutput, calls=%fused_computation.4 | convolution fusion | flops 819462144 | bytes 41418848 | tf_op jit(solution)/shard_map/isr,sicq->ricq/dot_general | solution.py:37
  248.3 16.7 %copy.82 = bf16[256,16,6,256]{3,1,2,0:T(8,128)(2,1)} copy(bf16[256,16,6,256]{0,3,2,1:T(8,128)(2,1)} %fusion) | data formatting | bytes 25165824 | tf_op jit(solution)/shard_map/convert_element_type | solution.py:41
  265.0 0.1 copy.69
  265.1 0.1 iota_compare_fusion
  265.2 1.0 copy-done
  266.2 0.9 fusion.26
  267.2 0.1 select_reduce_fusion
  267.3 0.1 broadcast_and_fusion
  267.5 95.1 %reduce-scatter.2.cloned.1.call-done = bf16[16,16,6,256]{3,1,2,0:T(8,128)(2,1)} async-done(((bf16[256,16,6,256]{3,1,2,0:T(8,128)(2,1)}), bf16[16,16,6,256]{3,1,2,0:T(8,128)(2,1)}) %reduce-scatter.2.cloned.1.call-update) | async-done | bytes 786448 | tf_op jit(solution)/shard_map/reduce_scatter | solution.py:40
  362.6 3.9 %multiply_select_fusion = f32[16,16,6,256]{3,1,2,0:T(8,128)} fusion(bf16[16,16,6,256]{3,1,2,0:T(8,128)(2,1)} %reduce-scatter.2.cloned.1.call-done, f32[16,16]{1,0:T(8,128)S(1)} %broadcast_divide_fusion, f32[16,16,256]{2,1,0:T(8,128)S(1)} %get-tuple-element.13, f32[16,16,256]{2,1,0:T(8,128)S(1)} %get-tuple-element.14, ...), kind=kLoop, calls=%fused_computation.16 | loop fusion | flops 7471104 | bytes 3433856 | tf_op jit(solution)/shard_map/jit(_where)/select_n | solution.py:58
  (24 shorter events, 0.2 us)
Async XLA Ops:
  6.5 4.2 %copy-start.3 = (s32[16,4]{0,1:T(4,128)S(1)}, s32[16,4]{0,1:T(4,128)}, u32[]{:S(2)}) copy-start(s32[16,4]{0,1:T(4,128)} %param.7) | copy-start | bytes 772
  6.5 62.8 %all-gather.4.cloned.1.call-start = ((), (), s32[]{:S(2)}) async-start(), calls=%async_computation.1 | async-start | bytes 8912896 | tf_op jit(solution)/shard_map/all_gather | solution.py:21
  7.3 145.2 %all-gather.6.cloned.1.call-start = ((), (), s32[]{:S(2)}) async-start(), calls=%async_computation.2 | async-start | bytes 8912896 | tf_op jit(solution)/shard_map/all_gather | solution.py:26
  10.7 205.4 %all-gather.8.cloned.1.call-start = ((), (), s32[]{:S(2)}) async-start(), calls=%async_computation.3 | async-start | bytes 8912896 | tf_op jit(solution)/shard_map/all_gather | solution.py:30
  152.4 7.0 %copy-start.2 = (s32[16,6]{0,1:T(8,128)S(1)}, s32[16,6]{0,1:T(8,128)}, u32[]{:S(2)}) copy-start(s32[16,6]{0,1:T(8,128)} %param.9) | copy-start | bytes 1156
  152.4 7.3 %copy-start.1 = (bf16[64,4096]{1,0:T(8,128)(2,1)S(1)}, bf16[64,4096]{1,0:T(8,128)(2,1)}, u32[]{:S(2)}) copy-start(bf16[64,4096]{1,0:T(8,128)(2,1)} %param.5) | copy-start | bytes 1572868
  159.4 203.3 %reduce-scatter.2.cloned.1.call-start = ((), (), s32[]{:S(2)}) async-start(), calls=%async_computation.4 | async-start | bytes 13369344 | tf_op jit(solution)/shard_map/reduce_scatter | solution.py:40
  265.0 1.2 copy-start
Sparse Core Ops, SparseCore 0:
  9.2 60.1 all-gather.3
  71.8 80.6 all-gather.5
  159.5 56.6 all-gather.7
  265.2 97.4 reduce-scatter.1
where the time goes:
time: 374 us; the launch traced here: 373 us
  waiting for transfers between devices  275 us (74%)
  local copies, waits for them, and re-layouts  42.2 us (11%)
  matrix products  34.9 us (9%)
  between operations  13.3 us (4%)
  other arithmetic  7.59 us (2%)
    reduce_scatter x1, waiting for transfers between devices, body(): lax.psum_scatter((left_terms + right_terms).astype(jnp.bfloat16), 'layer'...  95.1 us
    all_gather x1, waiting for transfers between devices, body(): lax.all_gather(half_blocks, 'layer', axis=0, tiled=True)  71.2 us
    all_gather x1, waiting for transfers between devices, body(): gathered = lax.all_gather(sample_matrix, 'var', axis=1, tiled=True)  58.3 us
    all_gather x1, waiting for transfers between devices, body(): all_products = lax.all_gather(local_products, 'var', axis=0, tiled=True)  49.6 us
    convert_element_type x1, local copies, waits for them, and re-layouts, body(): (left_terms + right_terms).astype(jnp.bfloat16)  16.7 us
    dot_general x1, matrix products, body(): jnp.einsum('isr,sicq->ricq', local_products, far_columns, preferred_eleme...  15.3 us
    dot_general x1, matrix products, body(): jnp.einsum('sir,icsq->ricq', own_columns, far_products, preferred_element...  12.7 us
    reshape x1, local copies, waits for them, and re-layouts, body(): gathered.reshape(per_layer, gathered.shape[1] // block_width, block_width)  7.79 us
  transfers between devices with their start and end apart: 4, of which 4 were waited for; matrix products, arithmetic and copies ran while one was open for 6% of the time, Pallas kernels for 0%

commit v1 on v0

v1 whole, which is shorter than its diff:
```python
import jax
import jax.numpy as jnp
from jax import lax
from jax.experimental import pallas as pl
from jax.experimental.pallas import tpu as pltpu
from jax.sharding import PartitionSpec as P

step_size = 0.5
penalty = 0.04

NZ, NC, NY, NX = 8, 2, 4, 4
BLOCKS = 16
SAMP = 64
HALF = 128
SLOTS = 6
CHUNKS = 14
MESH = pl.DeviceIdType.MESH
bf16, f32 = jnp.bfloat16, jnp.float32

PARTS = (("x", 1), ("x", -1), ("y", 1), ("y", -1))


def kernel(x_ref, w_ref, pat_ref, cand_ref, out_ref,
           xg, pg0, pg1, wg, at, terms, fwd1, part, fwd2, m1, m23, n1, n23,
           x_rs, x_ss, xp_rs, xp_ss, w_rs, w_ss, p_rs, p_ss, pp_rs, pp_ss,
           m1_rs, m23_rs, n1_rs, n23_rs, t_ss, r_ss, own_sem):
    v = lax.axis_index("var")
    l = lax.axis_index("layer")
    z, core = v // NC, v % NC
    y, x = l // NX, l % NX
    here = {"x": x, "y": y}
    size = {"x": NX, "y": NY}

    def at_z(step):
        return {"var": ((z + step + NZ) % NZ) * NC + core, "layer": l}

    def at_xy(axis, step):
        if axis == "x":
            return {"var": v, "layer": y * NX + (x + step + NX) % NX}
        return {"var": v, "layer": ((y + step + NY) % NY) * NX + x}

    partner = {"var": z * NC + (1 - core), "layer": l}

    barrier = pltpu.get_barrier_semaphore()
    greeted = [at_z(1), at_z(-1), partner, at_xy("x", 1), at_xy("x", -1), at_xy("y", 1), at_xy("y", -1)]
    for device in greeted:
        pl.semaphore_signal(barrier, inc=1, device_id=device, device_id_type=MESH)

    for j in range(BLOCKS):
        for h in range(2):
            start = (j * 2 + h) * HALF
            xg[v * BLOCKS + j, h] = x_ref[:, start:start + HALF]
    own_w = pltpu.make_async_copy(w_ref, wg.at[l], own_sem)
    own_w.start()
    pl.semaphore_wait(barrier, len(greeted))

    def push(src, dst, ss, rs, device):
        pltpu.make_async_remote_copy(src_ref=src, dst_ref=dst, send_sem=ss, recv_sem=rs,
                                     device_id=device, device_id_type=MESH).start()

    def arrived(ref, sem):
        pltpu.make_async_copy(ref, ref, sem).wait()

    def x_piece(vsrc, p):
        return xg.at[pl.ds(vsrc * BLOCKS + p * 4, 4)]

    def x_ring(vsrc, p, sign, hop):
        ref = x_piece(vsrc, p)
        push(ref, ref, x_ss, x_rs.at[0 if sign > 0 else 1, hop - 1, p], at_z(sign))

    def x_hop(h):
        for p in range(4):
            for sign in (1, -1):
                last = 4 if (p < 2) == (sign > 0) else 3
                if h > last:
                    continue
                vsrc = ((z - sign * h + NZ) % NZ) * NC + core
                ref = x_piece(vsrc, p)
                arrived(ref, x_rs.at[0 if sign > 0 else 1, h - 1, p])
                if h < last:
                    x_ring(vsrc, p, sign, h + 1)
                push(ref, ref, xp_ss, xp_rs, partner)

    for p in range(4):
        for sign in (1, -1):
            x_ring(v, p, sign, 1)

    def w_piece(lsrc, q):
        return wg.at[lsrc, q]

    def w_send(lsrc, q, axis, step):
        ref = w_piece(lsrc, q)
        push(ref, ref, w_ss, w_rs.at[q, lsrc], at_xy(axis, step))

    def w_wait(lsrc, q):
        arrived(w_piece(lsrc, q), w_rs.at[q, lsrc])

    def other(axis):
        return "y" if axis == "x" else "x"

    def l_at(first, a, second, b):
        pos = dict(here)
        pos[first] = (pos[first] + a + 4) % 4
        pos[second] = (pos[second] + b + 4) % 4
        return pos["y"] * NX + pos["x"]

    def each():
        for q, (d1, s) in enumerate(PARTS):
            yield q, d1, other(d1), s

    own_w.wait()
    for q, d1, d2, s in each():
        for step in (1, -1):
            w_send(l, q, d1, step)
    for q, d1, d2, s in each():
        for step in (1, -1):
            w_send(l, q, d2, step)
    push(xg.at[pl.ds(v * BLOCKS, BLOCKS)], xg.at[pl.ds(v * BLOCKS, BLOCKS)], xp_ss, xp_rs, partner)

    for q, d1, d2, s in each():
        for a in (-s, s):
            lsrc = l_at(d1, a, d2, 0)
            w_wait(lsrc, q)
            if a == -s:
                w_send(lsrc, q, d1, s)
            for step in (1, -1):
                w_send(lsrc, q, d2, step)
    x_hop(1)
    for q, d1, d2, s in each():
        for b in (-s, s):
            lsrc = l_at(d1, 0, d2, b)
            w_wait(lsrc, q)
            if b == -s:
                w_send(lsrc, q, d2, s)
    for q, d1, d2, s in each():
        lsrc = l_at(d1, 2, d2, 0)
        w_wait(lsrc, q)
        for step in (1, -1):
            w_send(lsrc, q, d2, step)
    x_hop(2)
    for a in (-1, 1, 2):
        for q, d1, d2, s in each():
            for b in (-s, s):
                lsrc = l_at(d1, a, d2, b)
                w_wait(lsrc, q)
                if b == -s:
                    w_send(lsrc, q, d2, s)
        if a == 1:
            x_hop(3)
    x_hop(4)
    arrived(xg.at[pl.ds(0, NZ * BLOCKS)], xp_rs)
    for a in (0, -1, 1, 2):
        for q, d1, d2, s in each():
            w_wait(l_at(d1, a, d2, 2), q)

    def product(i, carry):
        total = jnp.zeros((SAMP, 2 * HALF), f32)
        for k in range(4):
            j = pat_ref[i, k]
            cols = jnp.concatenate([xg[j, 0], xg[j, 1]], axis=1)
            rows = wg[:, i // 4, i % 4, k].reshape(2 * HALF, 2 * HALF)
            total += lax.dot_general(cols, rows, (((1,), (1,)), ((), ())), preferred_element_type=f32)
        result = total.astype(bf16)
        pg0[v * BLOCKS + i] = result[:, :HALF]
        pg1[v * BLOCKS + i] = result[:, HALF:]
        own = jnp.concatenate([xg[v * BLOCKS + i, 0], xg[v * BLOCKS + i, 1]], axis=1)
        both = jnp.concatenate([own.astype(f32), result.astype(f32)], axis=0)
        at[i] = both.T.astype(bf16)
        return carry

    lax.fori_loop(0, BLOCKS, product, 0)

    def p_piece(pg, vsrc, p):
        return pg.at[pl.ds(vsrc * BLOCKS + p * 8, 8)]

    def p_ring(qh, pg, vsrc, p, sign, hop):
        ref = p_piece(pg, vsrc, p)
        push(ref, ref, p_ss.at[qh], p_rs.at[qh, 0 if sign > 0 else 1, hop - 1, p], at_z(sign))

    def p_start(qh, pg):
        for p in range(2):
            for sign in (1, -1):
                p_ring(qh, pg, v, p, sign, 1)
        ref = pg.at[pl.ds(v * BLOCKS, BLOCKS)]
        push(ref, ref, pp_ss.at[qh], pp_rs.at[qh], partner)

    def p_hop(qh, pg, h):
        for p in range(2):
            for sign in (1, -1):
                last = 4 if (p == 0) == (sign > 0) else 3

                def step(p=p, sign=sign, last=last):
                    vsrc = ((z - sign * h + NZ) % NZ) * NC + core
                    ref = p_piece(pg, vsrc, p)
                    arrived(ref, p_rs.at[qh, 0 if sign > 0 else 1, h - 1, p])

                    @pl.when(h < last)
                    def _():
                        p_ring(qh, pg, vsrc, p, sign, h + 1)
                    push(ref, ref, pp_ss.at[qh], pp_rs.at[qh], partner)

                if last == 4:
                    step()
                else:
                    pl.when(h <= 3)(step)

        @pl.when(h == 4)
        def _():
            arrived(pg.at[pl.ds(0, NZ * BLOCKS)], pp_rs.at[qh])

    def place(axis, step):
        return (here[axis] + step + 4) % 4

    def stage0(u, qh, pg, own):
        slot = u % SLOTS
        for q, d1, d2, s in each():
            def one(i4, carry, q=q, d1=d1):
                i = q * 4 + i4
                if own:
                    j = v * BLOCKS + i
                else:
                    j = cand_ref[i, u - (3 if qh == 0 else 8)]
                right = jnp.concatenate([pg[j], xg[j, qh]], axis=0)
                term = jnp.dot(at[i], right, preferred_element_type=f32).astype(bf16)
                for a in range(4):
                    for b in range(4):
                        row = 16 * ((b * NX + a) if d1 == "x" else (a * NX + b))
                        terms[slot, q, a, b, i4] = term[row:row + 16]
                return carry

            for i4 in range(4):
                one(i4, 0)
            push(terms.at[slot, q, place(d1, 2)], m1.at[u, q], t_ss.at[slot], m1_rs.at[u], at_xy(d1, s))
            push(terms.at[slot, q, place(d1, -s)], m23.at[u, q, 0], t_ss.at[slot], m23_rs.at[u], at_xy(d1, -s))

    def stage1(u):
        slot = u % SLOTS
        arrived(m1.at[u], m1_rs.at[u])
        for q, d1, d2, s in each():
            fwd1[slot, q] = (terms[slot, q, place(d1, s)].astype(f32) + m1[u, q].astype(f32)).astype(bf16)
            push(fwd1.at[slot, q], m23.at[u, q, 1], t_ss.at[slot], m23_rs.at[u], at_xy(d1, s))

    def stage2(u):
        slot = u % SLOTS
        arrived(m23.at[u], m23_rs.at[u])
        for q, d1, d2, s in each():
            part[slot, q] = (terms[slot, q, place(d1, 0)].astype(f32) + m23[u, q, 0].astype(f32)
                             + m23[u, q, 1].astype(f32)).astype(bf16)
            push(part.at[slot, q, place(d2, 2)], n1.at[u, q], r_ss.at[slot], n1_rs.at[u], at_xy(d2, s))
            push(part.at[slot, q, place(d2, -s)], n23.at[u, q, 0], r_ss.at[slot], n23_rs.at[u], at_xy(d2, -s))

    def stage3(u):
        slot = u % SLOTS
        arrived(n1.at[u], n1_rs.at[u])
        for q, d1, d2, s in each():
            fwd2[slot, q] = (part[slot, q, place(d2, s)].astype(f32) + n1[u, q].astype(f32)).astype(bf16)
            push(fwd2.at[slot, q], n23.at[u, q, 1], r_ss.at[slot], n23_rs.at[u], at_xy(d2, s))

    def stage4(u):
        slot = u % SLOTS
        arrived(n23.at[u], n23_rs.at[u])
        for q, d1, d2, s in each():
            out_ref[u, pl.ds(q * 4, 4)] = (part[slot, q, place(d2, 0)].astype(f32) + n23[u, q, 0].astype(f32)
                                           + n23[u, q, 1].astype(f32))
        arrived(terms.at[slot, pl.ds(0, 3)], t_ss.at[slot])
        arrived(part.at[slot, pl.ds(0, 3)], r_ss.at[slot])

    def filled(u):
        return ((u >= 0) & (u < 2)) | ((u >= 4) & (u < CHUNKS))

    p_start(0, pg0)

    def turn(u, carry):
        pl.when(u == 0)(lambda: stage0(u, 0, pg0, True))
        pl.when(u == 1)(lambda: stage0(u, 1, pg1, True))
        pl.when((u >= 4) & (u < 9))(lambda: stage0(u, 0, pg0, False))
        pl.when((u >= 9) & (u < 14))(lambda: stage0(u, 1, pg1, False))
        pl.when(filled(u - 1))(lambda: stage1(u - 1))
        pl.when(filled(u - 2))(lambda: stage2(u - 2))
        pl.when(filled(u - 3))(lambda: stage3(u - 3))
        pl.when(filled(u - 4))(lambda: stage4(u - 4))
        pl.when(u < 4)(lambda: p_hop(0, pg0, u + 1))
        pl.when(u == 2)(lambda: p_start(1, pg1))
        pl.when((u >= 4) & (u < 8))(lambda: p_hop(1, pg1, u - 3))
        return carry

    lax.fori_loop(0, CHUNKS + 4, turn, 0)

    arrived(xg.at[pl.ds(0, 7 * BLOCKS)], x_ss)
    arrived(xg.at[pl.ds(0, 8 * BLOCKS)], xp_ss)
    arrived(wg.at[pl.ds(0, 15)], w_ss)
    for qh, pg in enumerate((pg0, pg1)):
        arrived(pg.at[pl.ds(0, 7 * BLOCKS)], p_ss.at[qh])
        arrived(pg.at[pl.ds(0, 8 * BLOCKS)], pp_ss.at[qh])


def step(sample_matrix, half, block_pattern, candidate_cols):
    vmem = pl.BlockSpec(memory_space=pltpu.VMEM)
    smem = pl.BlockSpec(memory_space=pltpu.SMEM)
    dma = pltpu.SemaphoreType.DMA
    scratch = [
        pltpu.VMEM((256, 2, SAMP, HALF), bf16),
        pltpu.VMEM((256, SAMP, HALF), bf16),
        pltpu.VMEM((256, SAMP, HALF), bf16),
        pltpu.VMEM((16, 4, 4, 4, 16, 256), bf16),
        pltpu.VMEM((BLOCKS, 256, 128), bf16),
        pltpu.VMEM((SLOTS, 4, 4, 4, 4, 16, HALF), bf16),
        pltpu.VMEM((SLOTS, 4, 4, 4, 16, HALF), bf16),
        pltpu.VMEM((SLOTS, 4, 4, 4, 16, HALF), bf16),
        pltpu.VMEM((SLOTS, 4, 4, 16, HALF), bf16),
        pltpu.VMEM((CHUNKS, 4, 4, 4, 16, HALF), bf16),
        pltpu.VMEM((CHUNKS, 4, 2, 4, 4, 16, HALF), bf16),
        pltpu.VMEM((CHUNKS, 4, 4, 16, HALF), bf16),
        pltpu.VMEM((CHUNKS, 4, 2, 4, 16, HALF), bf16),
        dma((2, 4, 4)), dma(()), dma(()), dma(()),
        dma((4, 16)), dma(()),
        dma((2, 2, 4, 2)), dma((2,)), dma((2,)), dma((2,)),
        dma((CHUNKS,)), dma((CHUNKS,)), dma((CHUNKS,)), dma((CHUNKS,)), dma((SLOTS,)), dma((SLOTS,)), dma(()),
    ]
    return pl.pallas_call(
        kernel,
        out_shape=jax.ShapeDtypeStruct((CHUNKS, BLOCKS, 16, HALF), f32),
        in_specs=[vmem, vmem, smem, smem],
        out_specs=vmem,
        scratch_shapes=scratch,
        compiler_params=pltpu.CompilerParams(
            collective_id=0, has_side_effects=True, vmem_limit_bytes=60 * 2 ** 20),
    )(sample_matrix, half, block_pattern, candidate_cols)


def body(sample_matrix, precision_blocks, block_pattern, block_counts, candidate_cols):
    layer_count = lax.axis_size("layer")
    layer_index = lax.axis_index("layer")
    rows_here, local_rows, stored, block_width = precision_blocks.shape
    per_layer = sample_matrix.shape[0]
    chosen_count = candidate_cols.shape[1]
    total_samples = per_layer * layer_count
    live_slots = jnp.arange(stored)[None, :] < block_counts[:, None]
    half_blocks = jnp.where(live_slots[None, :, :, None], precision_blocks, 0.0).astype(jnp.bfloat16)
    half = jnp.transpose(half_blocks, (1, 2, 0, 3)).reshape(4, 4, stored, rows_here, block_width)
    sums = step(sample_matrix, half, block_pattern, candidate_cols)
    first = jnp.transpose(sums[0:2], (2, 1, 0, 3)).reshape(rows_here, local_rows, 1, block_width)
    rest = jnp.transpose(sums[4:].reshape(2, 5, local_rows, rows_here, HALF), (3, 2, 1, 0, 4))
    rest = rest.reshape(rows_here, local_rows, 5, block_width)
    gradient = jnp.concatenate([first, rest], axis=2) / (2.0 * total_samples)
    global_rows = layer_index * rows_here + jnp.arange(rows_here)
    eye_mask = global_rows[:, None] == jnp.arange(block_width)[None, :]
    diagonal = jnp.sum(jnp.where(eye_mask[:, None, :], precision_blocks[:, :, 0, :], 0.0), axis=2)
    first_slot = jnp.arange(chosen_count) == 0
    diag_mask = eye_mask[:, None, None, :] & first_slot[None, None, :, None]
    gradient = gradient - jnp.where(diag_mask, (1.0 / diagonal)[:, :, None, None], 0.0)
    matches = (candidate_cols[:, :, None] == block_pattern[:, None, :]) & live_slots[:, None, :]
    previous = jnp.zeros(gradient.shape, jnp.float32)
    for slot_index in range(stored):
        previous = previous + jnp.where(
            matches[None, :, :, slot_index, None], precision_blocks[:, :, None, slot_index, :], 0.0
        )
    stepped = previous - step_size * gradient
    shrunk = jnp.sign(stepped) * jnp.maximum(jnp.abs(stepped) - step_size * penalty, 0.0)
    return jnp.where(diag_mask, stepped, shrunk)


def solution(mesh):
    placed = (
        P("layer", "var"),
        P("layer", "var", None, None),
        P("var", None),
        P("var"),
        P("var", None),
    )
    return jax.shard_map(
        body, mesh=mesh, in_specs=placed, out_specs=P("layer", "var", None, None), check_vma=False
    )
```

time: 374 us -> 172 us (0.46)
  waiting for transfers between devices: 275 us -> 0 us
  Pallas kernels: 0 us -> 155 us
  matrix products: 34.9 us -> 0 us
  local copies, waits for them, and re-layouts: 42.2 us -> 10.5 us
  between operations: 13.3 us -> 0.15 us
    all_gather x3 -> x0, waiting for transfers between devices: 179 us -> none  [the longest x1 71.2 us: body(): lax.all_gather(half_blocks, 'layer', axis=0, tiled=True)]
    pallas_call x0 -> x1, Pallas kernels: none -> 155 us  [step(): pl.pallas_call(kernel, out_shape=jax.ShapeDtypeStruct((CHUNKS, BLOCKS, 16...]
    reduce_scatter x1 -> x0, waiting for transfers between devices: 95.1 us -> none  [body(): lax.psum_scatter((left_terms + right_terms).astype(jnp.bfloat16), 'layer'...]
    dot_general x3 -> x0, matrix products: 34.9 us -> none  [the longest x1 15.3 us: body(): jnp.einsum('isr,sicq->ricq', local_products, far_columns, preferred_eleme...]
    convert_element_type x1 -> x0, local copies, waits for them, and re-layouts: 16.7 us -> none  [body(): (left_terms + right_terms).astype(jnp.bfloat16)]
    gather x3 -> x0, local copies, waits for them, and re-layouts: 14.1 us -> none  [the longest x1 5.9 us: body(): far_columns = jnp.take(column_blocks, candidate_cols, axis=1)]
    reshape x1 -> x2, local copies, waits for them, and re-layouts: 7.79 us -> 2.67 us  [the longest x1 2.46 us: body(): rest = rest.reshape(rows_here, local_rows, 5, block_width)]
  transfers between devices with their start and end apart: 4 -> 0, of which waited for: 4 -> 0; matrix products, arithmetic and copies ran while one was open for 6% -> 0% of each run, Pallas kernels for 0% -> 0%
where the time goes in v1:
time: 172 us; the launch traced here: 171 us
  Pallas kernels  155 us (90%)
  local copies, waits for them, and re-layouts  10.5 us (6%)
  other arithmetic  5.27 us (3%)
    pallas_call x1, Pallas kernels, step(): pl.pallas_call(kernel, out_shape=jax.ShapeDtypeStruct((CHUNKS, BLOCKS, 16...  155 us

profile of v1, /device:TPU:1, one launch (start us, length us, event | category | flops | bytes accessed | tf_op | source)
XLA Modules:
  0.0 171.0 jit_solution(15545247928090619254)
XLA Ops:
  0.0 0.0 copy-start.3
  0.0 0.0 copy-start.2
  0.0 0.7 iota_compare_fusion.1
  0.7 0.1 copy.15
  0.8 1.6 fusion.3
  2.4 1.1 copy.16
  3.5 0.0 copy-done.3
  3.5 0.7 copy.17.pat_ref
  4.1 0.0 copy-done.2
  4.1 0.7 copy.18.cand_ref
  4.8 155.0 %shard_map.55 = f32[14,16,16,128]{3,2,1,0:T(8,128)} custom-call(bf16[64,4096]{1,0:T(8,128)(2,1)} %x_ref.1, bf16[4,4,4,16,256]{4,3,2,1,0:T(8,128)(2,1)} %bitcast.30, s32[16,4]{1,0:T(8,128)} %copy.17.pat_ref, s32[16,6]{1,0:T(8,128)} %copy.18.cand_ref), custom_call_target="tpu_custom_call" | custom-call | tf_op jit(solution)/shard_map/pallas_call | solution.py:320
  159.9 0.0 slice-start
  159.9 1.3 slice-done
  161.2 2.1 %copy.20 = f32[16,16,5,2,128]{4,3,1,2,0:T(2,128)} copy(f32[16,16,5,2,128]{4,0,1,2,3:T(8,128)S(1)} %bitcast.29) | data formatting | bytes 2621440 | tf_op jit(solution)/shard_map/transpose | solution.py:343
  163.3 0.0 copy-start
  163.3 2.5 %reshape.108 = f32[16,16,5,256]{3,1,2,0:T(8,128)S(1)} reshape(f32[16,16,5,2,128]{4,3,1,2,0:T(2,128)} %copy.20) | data formatting | bytes 2621440 | tf_op jit(solution)/shard_map/reshape | solution.py:344
  165.7 0.0 copy-done
  165.8 0.0 copy-start.1
  165.8 0.2 copy.19
  166.0 0.2 reshape.106
  166.2 0.1 iota_compare_fusion
  166.3 0.7 copy-done.1
  167.0 0.9 fusion.4
  167.9 0.1 select_reduce_fusion
  168.2 0.1 broadcast_and_fusion
  168.3 2.7 %multiply_select_fusion = f32[16,16,6,256]{3,1,2,0:T(8,128)} fusion(f32[16,16,5,256]{3,1,2,0:T(8,128)S(1)} %reshape.108, f32[16,16,1,256]{3,1,2,0:T(8,128)S(1)} %bitcast.31, f32[16,16]{1,0:T(8,128)S(1)} %broadcast_divide_fusion, f32[16,16,256]{2,1,0:T(8,128)S(1)} %get-tuple-element.13, f32[16,16,256]{2,1,0:T(8,128)S(1)} %get-tuple-element.14, ...), kind=kLoop, calls=%fused_computation.4 | loop fusion | flops 7471104 | bytes 4220288 | tf_op jit(solution)/shard_map/jit(_where)/select_n | solution.py:360
  (8 shorter events, 0.1 us)
Async XLA Ops:
  0.0 3.5 %copy-start.3 = (s32[16,4]{0,1:T(4,128)S(1)}, s32[16,4]{0,1:T(4,128)}, u32[]{:S(2)}) copy-start(s32[16,4]{0,1:T(4,128)} %param.7) | copy-start | bytes 772
  0.0 4.1 %copy-start.2 = (s32[16,6]{0,1:T(8,128)S(1)}, s32[16,6]{0,1:T(8,128)}, u32[]{:S(2)}) copy-start(s32[16,6]{0,1:T(8,128)} %param.9) | copy-start | bytes 1156
  159.9 1.3 slice-start
  163.3 2.5 %copy-start = (f32[14,16,16,128]{3,2,1,0:T(8,128)S(1)}, f32[14,16,16,128]{3,2,1,0:T(8,128)}, u32[]{:S(2)}) copy-start(f32[14,16,16,128]{3,2,1,0:T(8,128)} %shard_map.55) | copy-start | bytes 5505028
  165.8 1.2 copy-start.1

commit v2 on v1

v2 whole, which is shorter than its diff:
```python
import jax
import jax.numpy as jnp
from jax import lax
from jax.experimental import pallas as pl
from jax.experimental.pallas import tpu as pltpu
from jax.sharding import PartitionSpec as P

step_size = 0.5
penalty = 0.04

NZ, NC, NY, NX = 8, 2, 4, 4
BLOCKS = 16
SAMP = 64
HALF = 128
QUARTER = 64
TOTAL = 1024
CHUNKS = 12
SLOTS = 8
LAGS = (1, 3, 5, 7)
MESH = pl.DeviceIdType.MESH
bf16, f32 = jnp.bfloat16, jnp.float32


PARTS = (("x", 1), ("x", -1), ("y", 1), ("y", -1))


def turned(value):
    return pltpu.roll(value.astype(f32), QUARTER, axis=value.ndim - 1)


def low_lanes(shape):
    return lax.broadcasted_iota(jnp.int32, shape, len(shape) - 1) < QUARTER


def kernel(x_ref, w_ref, pat_ref, count_ref, cand_ref, out_ref,
           xg, pga, pgb, pg1, own_p, wg, wt, at, hold, terms, fwd1, part, fwd2, m1, m23, n1, n23,
           x_rs, x_ss, xp_rs, xp_ss, w_rs, w_ss, p_rs, p_ss, pp_rs, pp_ss,
           m1_rs, m23_rs, n1_rs, n23_rs, t_ss, r_ss):
    v = lax.axis_index("var")
    l = lax.axis_index("layer")
    z, core = v // NC, v % NC
    y, x = l // NX, l % NX
    here = {"x": x, "y": y}

    def at_z(step):
        return {"var": ((z + step + NZ) % NZ) * NC + core, "layer": l}

    def at_xy(axis, step):
        if axis == "x":
            return {"var": v, "layer": y * NX + (x + step + NX) % NX}
        return {"var": v, "layer": ((y + step + NY) % NY) * NX + x}

    partner = {"var": z * NC + (1 - core), "layer": l}

    barrier = pltpu.get_barrier_semaphore()
    greeted = [at_z(1), at_z(-1), partner, at_xy("x", 1), at_xy("x", -1), at_xy("y", 1), at_xy("y", -1)]
    for device in greeted:
        pl.semaphore_signal(barrier, inc=1, device_id=device, device_id_type=MESH)

    for j in range(BLOCKS):
        for h in range(2):
            start = (j * 2 + h) * HALF
            xg[v * BLOCKS + j, h] = x_ref[:, start:start + HALF]
    pl.semaphore_wait(barrier, len(greeted))

    def push(src, dst, ss, rs, device):
        pltpu.make_async_remote_copy(src_ref=src, dst_ref=dst, send_sem=ss, recv_sem=rs,
                                     device_id=device, device_id_type=MESH).start()

    def arrived(ref, sem):
        pltpu.make_async_copy(ref, ref, sem).wait()

    def x_piece(vsrc, p):
        return xg.at[pl.ds(vsrc * BLOCKS + p * 4, 4)]

    def x_ring(vsrc, p, sign, hop):
        ref = x_piece(vsrc, p)
        push(ref, ref, x_ss, x_rs.at[0 if sign > 0 else 1, hop - 1, p], at_z(sign))

    def x_hop(h):
        for p in range(4):
            for sign in (1, -1):
                last = 4 if (p < 2) == (sign > 0) else 3
                if h > last:
                    continue
                vsrc = ((z - sign * h + NZ) % NZ) * NC + core
                ref = x_piece(vsrc, p)
                arrived(ref, x_rs.at[0 if sign > 0 else 1, h - 1, p])
                if h < last:
                    x_ring(vsrc, p, sign, h + 1)
                push(ref, ref, xp_ss, xp_rs, partner)

    for p in range(4):
        for sign in (1, -1):
            x_ring(v, p, sign, 1)

    def w_piece(lsrc, q):
        return wg.at[lsrc, q]

    def w_send(lsrc, q, axis, step):
        ref = w_piece(lsrc, q)
        push(ref, ref, w_ss, w_rs.at[q, lsrc], at_xy(axis, step))

    def w_wait(lsrc, q):
        arrived(w_piece(lsrc, q), w_rs.at[q, lsrc])

    def other(axis):
        return "y" if axis == "x" else "x"

    def l_at(first, a, second, b):
        pos = dict(here)
        pos[first] = (pos[first] + a + 4) % 4
        pos[second] = (pos[second] + b + 4) % 4
        return pos["y"] * NX + pos["x"]

    def each():
        for q, (d1, s) in enumerate(PARTS):
            yield q, d1, other(d1), s

    for q, d1, d2, s in each():
        def load(i4, carry, q=q):
            i = q * 4 + i4
            for k in range(4):
                rows = w_ref[:, i, k, :]
                wt[i, k] = rows
                wg[l, q, i4, k] = jnp.where(k < count_ref[i], rows, 0.0).astype(bf16)
            return carry

        lax.fori_loop(0, 4, load, 0)
        for step in (1, -1):
            w_send(l, q, d1, step)
    for q, d1, d2, s in each():
        for step in (1, -1):
            w_send(l, q, d2, step)
    push(xg.at[pl.ds(v * BLOCKS, BLOCKS)], xg.at[pl.ds(v * BLOCKS, BLOCKS)], xp_ss, xp_rs, partner)

    for q, d1, d2, s in each():
        for a in (-s, s):
            lsrc = l_at(d1, a, d2, 0)
            w_wait(lsrc, q)
            if a == -s:
                w_send(lsrc, q, d1, s)
            for step in (1, -1):
                w_send(lsrc, q, d2, step)
    x_hop(1)
    for q, d1, d2, s in each():
        for b in (-s, s):
            lsrc = l_at(d1, 0, d2, b)
            w_wait(lsrc, q)
            if b == -s:
                w_send(lsrc, q, d2, s)
    for q, d1, d2, s in each():
        lsrc = l_at(d1, 2, d2, 0)
        w_wait(lsrc, q)
        for step in (1, -1):
            w_send(lsrc, q, d2, step)
    x_hop(2)
    for a in (-1, 1, 2):
        for q, d1, d2, s in each():
            for b in (-s, s):
                lsrc = l_at(d1, a, d2, b)
                w_wait(lsrc, q)
                if b == -s:
                    w_send(lsrc, q, d2, s)
        if a == 1:
            x_hop(3)
    x_hop(4)
    arrived(xg.at[pl.ds(0, NZ * BLOCKS)], xp_rs)
    for a in (0, -1, 1, 2):
        for q, d1, d2, s in each():
            w_wait(l_at(d1, a, d2, 2), q)

    def product(i, carry):
        total = jnp.zeros((SAMP, 2 * HALF), f32)
        for k in range(4):
            j = pat_ref[k, i]
            cols = jnp.concatenate([xg[j, 0], xg[j, 1]], axis=1)
            rows = wg[:, i // 4, i % 4, k].reshape(2 * HALF, 2 * HALF)
            total += lax.dot_general(cols, rows, (((1,), (1,)), ((), ())), preferred_element_type=f32)
        result = total.astype(bf16)
        left = total[:, :HALF]
        other_half = turned(left)
        low = low_lanes((SAMP // 2, HALF))
        pga[v * BLOCKS + i] = jnp.where(low, left[:SAMP // 2], other_half[SAMP // 2:]).astype(bf16)
        pgb[v * BLOCKS + i] = jnp.where(low, other_half[:SAMP // 2], left[SAMP // 2:]).astype(bf16)
        own_p[i] = result[:, :HALF]
        pg1[v * BLOCKS + i] = result[:, HALF:]
        own = jnp.concatenate([xg[v * BLOCKS + i, 0], xg[v * BLOCKS + i, 1]], axis=1)
        both = jnp.concatenate([own.astype(f32), result.astype(f32)], axis=0)
        at[i] = both.T.astype(bf16)
        return carry

    lax.fori_loop(0, BLOCKS, product, 0)

    gathers = (pga, pgb, pg1)

    def p_piece(g, vsrc, p):
        return gathers[g].at[pl.ds(vsrc * BLOCKS + p * 8, 8)]

    def p_ring(g, vsrc, p, sign, hop):
        ref = p_piece(g, vsrc, p)
        push(ref, ref, p_ss.at[g], p_rs.at[g, 0 if sign > 0 else 1, hop - 1, p], at_z(sign))

    def p_start(g):
        for p in range(2):
            for sign in (1, -1):
                p_ring(g, v, p, sign, 1)
        ref = gathers[g].at[pl.ds(v * BLOCKS, BLOCKS)]
        push(ref, ref, pp_ss.at[g], pp_rs.at[g], partner)

    def p_hop(g, h):
        for p in range(2):
            for sign in (1, -1):
                last = 4 if (p == 0) == (sign > 0) else 3
                if h > last:
                    continue
                vsrc = ((z - sign * h + NZ) % NZ) * NC + core
                ref = p_piece(g, vsrc, p)
                arrived(ref, p_rs.at[g, 0 if sign > 0 else 1, h - 1, p])
                if h < last:
                    p_ring(g, vsrc, p, sign, h + 1)
                push(ref, ref, pp_ss.at[g], pp_rs.at[g], partner)
        if h == 4:
            arrived(gathers[g].at[pl.ds(0, NZ * BLOCKS)], pp_rs.at[g])

    def place(axis, step):
        return (here[axis] + step + 4) % 4

    def right_own(u, i):
        if u == 0:
            return jnp.concatenate([own_p[i], xg[v * BLOCKS + i, 0]], axis=0)
        return jnp.concatenate([pg1[v * BLOCKS + i], xg[v * BLOCKS + i, 1]], axis=0)

    def right_pair(u, i, second):
        base = 2 * u - (7 if second else 3)
        j, k = cand_ref[base, i], cand_ref[base + 1, i]
        pg = pgb if second else pga
        low = low_lanes((SAMP // 2, HALF))
        pj, pk, xj, xk = pg[j], pg[k], xg[j, 0], xg[k, 0]
        top = jnp.where(low, pj.astype(f32), turned(pk))
        bottom = jnp.where(low, turned(pj), pk.astype(f32))
        low = low_lanes((SAMP, HALF))
        if second:
            cols = jnp.where(low, turned(xj), xk.astype(f32))
        else:
            cols = jnp.where(low, xj.astype(f32), turned(xk))
        return jnp.concatenate([top, bottom, cols], axis=0).astype(bf16)

    def right_five(u, i):
        j = cand_ref[5, i]
        pa, pb = pga[j], pgb[j]
        low = low_lanes((SAMP // 2, HALF))
        top = jnp.where(low, pa.astype(f32), turned(pb))
        bottom = jnp.where(low, turned(pa), pb.astype(f32))
        return jnp.concatenate([top.astype(bf16), bottom.astype(bf16), xg[j, 0]], axis=0)

    def right_second(u, i):
        j = cand_ref[u - 6, i]
        return jnp.concatenate([pg1[j], xg[j, 1]], axis=0)

    def stage0(u, right):
        slot = u % SLOTS
        for q, d1, d2, s in each():
            for i4 in range(4):
                i = q * 4 + i4
                term = jnp.dot(at[i], right(u, i), preferred_element_type=f32).astype(bf16)
                for a in range(4):
                    for b in range(4):
                        row = 16 * ((b * NX + a) if d1 == "x" else (a * NX + b))
                        terms[slot, q, a, b, i4] = term[row:row + 16]
            push(terms.at[slot, q, place(d1, 2)], m1.at[u, q], t_ss.at[slot], m1_rs.at[u], at_xy(d1, s))
            push(terms.at[slot, q, place(d1, -s)], m23.at[u, q, 0], t_ss.at[slot], m23_rs.at[u], at_xy(d1, -s))

    def stage1(u):
        slot = u % SLOTS
        arrived(m1.at[u], m1_rs.at[u])
        for q, d1, d2, s in each():
            fwd1[slot, q] = (terms[slot, q, place(d1, s)].astype(f32) + m1[u, q].astype(f32)).astype(bf16)
            push(fwd1.at[slot, q], m23.at[u, q, 1], t_ss.at[slot], m23_rs.at[u], at_xy(d1, s))

    def stage2(u):
        slot = u % SLOTS
        arrived(m23.at[u], m23_rs.at[u])
        for q, d1, d2, s in each():
            part[slot, q] = (terms[slot, q, place(d1, 0)].astype(f32) + m23[u, q, 0].astype(f32)
                             + m23[u, q, 1].astype(f32)).astype(bf16)
            push(part.at[slot, q, place(d2, 2)], n1.at[u, q], r_ss.at[slot], n1_rs.at[u], at_xy(d2, s))
            push(part.at[slot, q, place(d2, -s)], n23.at[u, q, 0], r_ss.at[slot], n23_rs.at[u], at_xy(d2, -s))

    def stage3(u):
        slot = u % SLOTS
        arrived(n1.at[u], n1_rs.at[u])
        for q, d1, d2, s in each():
            fwd2[slot, q] = (part[slot, q, place(d2, s)].astype(f32) + n1[u, q].astype(f32)).astype(bf16)
            push(fwd2.at[slot, q], n23.at[u, q, 1], r_ss.at[slot], n23_rs.at[u], at_xy(d2, s))

    def finish(i, c, qh, total):
        columns = pl.ds(qh * HALF, HALF)
        j = cand_ref[c, i]
        live = count_ref[i]
        slot, found = 0, 0
        for k in range(4):
            match = jnp.where((pat_ref[k, i] == j) & (k < live), 1, 0)
            slot, found = slot + k * match, found + match
        previous = jnp.where(found > 0, wt[i, slot, :, columns], 0.0)
        stepped = previous - step_size * (total * (1.0 / (2.0 * TOTAL)))
        size = jnp.maximum(jnp.abs(stepped) - step_size * penalty, 0.0)
        result = jnp.where(stepped < 0, -size, size)
        if isinstance(c, int) and c == 0:
            rows = l * 16 + lax.broadcasted_iota(jnp.int32, (16, HALF), 0)
            cols = qh * HALF + lax.broadcasted_iota(jnp.int32, (16, HALF), 1)
            on = rows == cols
            diagonal = jnp.where(on, wt[i, 0, :, columns], 1.0)
            result = jnp.where(on, stepped + step_size * (1.0 / diagonal), result)
        out_ref[:, c, i, columns] = result

    def stage4(u, kind):
        slot = u % SLOTS
        arrived(n23.at[u], n23_rs.at[u])
        low = low_lanes((16, HALF))
        for q, d1, d2, s in each():
            for i4 in range(4):
                i = q * 4 + i4
                total = (part[slot, q, place(d2, 0), i4].astype(f32) + n23[u, q, 0, i4].astype(f32)
                         + n23[u, q, 1, i4].astype(f32))
                if kind == "own":
                    finish(i, 0, u, total)
                elif kind == "first":
                    hold[u - 2, i] = total
                elif kind == "pair":
                    before = hold[u - 4, i]
                    finish(i, 2 * u - 7, 0, jnp.where(low, before, turned(total)))
                    finish(i, 2 * u - 6, 0, jnp.where(low, turned(before), total))
                elif kind == "five":
                    finish(i, 5, 0, total)
                else:
                    finish(i, u - 6, 1, total)
        arrived(terms.at[slot, pl.ds(0, 3)], t_ss.at[slot])
        arrived(part.at[slot, pl.ds(0, 3)], r_ss.at[slot])

    p_start(0)
    stage0(0, right_own)
    stage0(1, right_own)
    p_hop(0, 1)
    stage1(0)
    p_hop(0, 2)
    stage1(1)
    p_hop(0, 3)
    p_start(1)
    stage2(0)
    p_hop(0, 4)
    stage2(1)

    def turn(u, carry):
        def when(low, high, what):
            pl.when((u >= low) & (u < high))(what)

        def hops(*steps):
            def run():
                for g, h in steps:
                    p_hop(g, h)
                    if (g, h) == (1, 3):
                        p_start(2)
            return run

        when(4, 5, hops((1, 4)))
        when(7, 8, hops((2, 4)))
        when(2, 4, lambda: stage0(u, lambda u, i: right_pair(u, i, False)))
        when(4, 6, lambda: stage0(u, lambda u, i: right_pair(u, i, True)))
        when(6, 7, lambda: stage0(u, right_five))
        when(7, 12, lambda: stage0(u, right_second))
        a, b, c, d = LAGS
        when(2 + a, 12 + a, lambda: stage1(u - a))
        when(2 + b, 12 + b, lambda: stage2(u - b))
        when(c, 12 + c, lambda: stage3(u - c))
        when(d, d + 1, lambda: stage4(0, "own"))
        when(d + 1, d + 2, lambda: stage4(1, "own"))
        when(d + 2, d + 4, lambda: stage4(u - d, "first"))
        when(d + 4, d + 6, lambda: stage4(u - d, "pair"))
        when(d + 6, d + 7, lambda: stage4(u - d, "five"))
        when(d + 7, d + 12, lambda: stage4(u - d, "second"))
        when(2, 3, hops((1, 1), (1, 2)))
        when(3, 4, hops((1, 3)))
        when(4, 5, hops((2, 1)))
        when(5, 6, hops((2, 2)))
        when(6, 7, hops((2, 3)))
        return carry

    lax.fori_loop(2, CHUNKS + LAGS[3], turn, 0)

    arrived(xg.at[pl.ds(0, 7 * BLOCKS)], x_ss)
    arrived(xg.at[pl.ds(0, 8 * BLOCKS)], xp_ss)
    arrived(wg.at[pl.ds(0, 15)], w_ss)
    for g in range(3):
        arrived(gathers[g].at[pl.ds(0, 7 * BLOCKS)], p_ss.at[g])
        arrived(gathers[g].at[pl.ds(0, 8 * BLOCKS)], pp_ss.at[g])


def body(sample_matrix, precision_blocks, block_pattern, block_counts, candidate_cols):
    vmem = pl.BlockSpec(memory_space=pltpu.VMEM)
    smem = pl.BlockSpec(memory_space=pltpu.SMEM)
    dma = pltpu.SemaphoreType.DMA
    scratch = [
        pltpu.VMEM((256, 2, SAMP, HALF), bf16),
        pltpu.VMEM((256, SAMP // 2, HALF), bf16),
        pltpu.VMEM((256, SAMP // 2, HALF), bf16),
        pltpu.VMEM((256, SAMP, HALF), bf16),
        pltpu.VMEM((BLOCKS, SAMP, HALF), bf16),
        pltpu.VMEM((16, 4, 4, 4, 16, 256), bf16),
        pltpu.VMEM((BLOCKS, 4, 16, 256), f32),
        pltpu.VMEM((BLOCKS, 256, 128), bf16),
        pltpu.VMEM((2, BLOCKS, 16, HALF), f32),
        pltpu.VMEM((SLOTS, 4, 4, 4, 4, 16, HALF), bf16),
        pltpu.VMEM((SLOTS, 4, 4, 4, 16, HALF), bf16),
        pltpu.VMEM((SLOTS, 4, 4, 4, 16, HALF), bf16),
        pltpu.VMEM((SLOTS, 4, 4, 16, HALF), bf16),
        pltpu.VMEM((CHUNKS, 4, 4, 4, 16, HALF), bf16),
        pltpu.VMEM((CHUNKS, 4, 2, 4, 4, 16, HALF), bf16),
        pltpu.VMEM((CHUNKS, 4, 4, 16, HALF), bf16),
        pltpu.VMEM((CHUNKS, 4, 2, 4, 16, HALF), bf16),
        dma((2, 4, 4)), dma(()), dma(()), dma(()),
        dma((4, 16)), dma(()),
        dma((3, 2, 4, 2)), dma((3,)), dma((3,)), dma((3,)),
        dma((CHUNKS,)), dma((CHUNKS,)), dma((CHUNKS,)), dma((CHUNKS,)), dma((SLOTS,)), dma((SLOTS,)),
    ]
    updated = pl.pallas_call(
        kernel,
        out_shape=jax.ShapeDtypeStruct((16, 6, BLOCKS, 2 * HALF), f32),
        in_specs=[vmem, vmem, smem, smem, smem],
        out_specs=vmem,
        scratch_shapes=scratch,
        compiler_params=pltpu.CompilerParams(
            collective_id=0, has_side_effects=True, vmem_limit_bytes=60 * 2 ** 20),
    )(sample_matrix, precision_blocks, block_pattern.T, block_counts, candidate_cols.T)
    return jnp.transpose(updated, (0, 2, 1, 3))


def solution(mesh):
    placed = (
        P("layer", "var"),
        P("layer", "var", None, None),
        P("var", None),
        P("var"),
        P("var", None),
    )
    return jax.shard_map(
        body, mesh=mesh, in_specs=placed, out_specs=P("layer", "var", None, None), check_vma=False
    )
```

time: 172 us -> 163 us (0.948)
  local copies, waits for them, and re-layouts: 10.5 us -> 2.71 us
  other arithmetic: 5.27 us -> 0 us
  Pallas kernels: 155 us -> 160 us
    pallas_call x1, Pallas kernels: 155 us -> 160 us  [body(): pl.pallas_call(kernel, out_shape=jax.ShapeDtypeStruct((16, 6, BLOCKS, 2 *...]
    transpose x4 -> x0, local copies, waits for them, and re-layouts: 3.38 us -> none  [the longest x1 2.07 us: body(): jnp.transpose(sums[4:].reshape(2, 5, local_rows, rows_here, HALF), (3, 2,...]
    select_n x1 -> x0, other arithmetic: 2.72 us -> none  [body(): return jnp.where(diag_mask, stepped, shrunk)]
    reshape x2 -> x0, local copies, waits for them, and re-layouts: 2.67 us -> none  [the longest x1 2.46 us: body(): rest = rest.reshape(rows_here, local_rows, 5, block_width)]
    slice x3 -> x0, local copies, waits for them, and re-layouts: 2.25 us -> none  [the longest x2 1.31 us: body(): sums[4:].reshape(2, 5, local_rows, rows_here, HALF)]
where the time goes in v2:
time: 163 us
  Pallas kernels  160 us (98%)
  local copies, waits for them, and re-layouts  2.71 us (2%)
    pallas_call x1, Pallas kernels, body(): pl.pallas_call(kernel, out_shape=jax.ShapeDtypeStruct((16, 6, BLOCKS, 2 *...  160 us

profile of v2, /device:TPU:1, one launch (start us, length us, event | category | flops | bytes accessed | tf_op | source)
XLA Modules:
  0.0 162.6 jit_solution(7604779285058733985)
XLA Ops:
  0.0 159.9 %shard_map.55 = f32[16,6,16,256]{3,2,1,0:T(8,128)} custom-call(bf16[64,4096]{1,0:T(8,128)(2,1)} %x_ref.1, f32[16,16,4,256]{3,2,1,0:T(4,128)} %w_ref.1, s32[4,16]{1,0:T(4,128)} %bitcast.5, s32[16]{0:T(128)} %count_ref.1, s32[6,16]{1,0:T(8,128)} %bitcast.4), custom_call_target="tpu_custom_call" | custom-call | tf_op jit(solution)/shard_map/pallas_call | solution.py:426
  159.9 2.7 %copy.7 = f32[16,16,6,256]{3,1,2,0:T(8,128)} copy(f32[16,16,6,256]{3,1,2,0:T(8,128)} %bitcast.3) | data formatting | bytes 3145728

commit v3 on v2

--- a/solution.py
+++ b/solution.py
@@ -15,6 +15,7 @@
 QUARTER = 64
 TOTAL = 1024
 CHUNKS = 12
+PIECES = 4
 SLOTS = 8
 LAGS = (1, 3, 5, 7)
 MESH = pl.DeviceIdType.MESH
@@ -77,8 +78,8 @@
         ref = x_piece(vsrc, p)
         push(ref, ref, x_ss, x_rs.at[0 if sign > 0 else 1, hop - 1, p], at_z(sign))
 
-    def x_hop(h):
-        for p in range(4):
+    def x_hop(h, pieces=range(4)):
+        for p in pieces:
             for sign in (1, -1):
                 last = 4 if (p < 2) == (sign > 0) else 3
                 if h > last:
@@ -134,36 +135,45 @@
             w_send(l, q, d2, step)
     push(xg.at[pl.ds(v * BLOCKS, BLOCKS)], xg.at[pl.ds(v * BLOCKS, BLOCKS)], xp_ss, xp_rs, partner)
 
-    for q, d1, d2, s in each():
-        for a in (-s, s):
-            lsrc = l_at(d1, a, d2, 0)
+    def w_first(parts=PARTS):
+        for q, d1, d2, s in each():
+            if PARTS[q] not in parts:
+                continue
+            for a in (-s, s):
+                lsrc = l_at(d1, a, d2, 0)
+                w_wait(lsrc, q)
+                if a == -s:
+                    w_send(lsrc, q, d1, s)
+                for step in (1, -1):
+                    w_send(lsrc, q, d2, step)
+
+    def w_long():
+        for q, d1, d2, s in each():
+            lsrc = l_at(d1, 2, d2, 0)
             w_wait(lsrc, q)
-            if a == -s:
-                w_send(lsrc, q, d1, s)
             for step in (1, -1):
                 w_send(lsrc, q, d2, step)
-    x_hop(1)
-    for q, d1, d2, s in each():
-        for b in (-s, s):
-            lsrc = l_at(d1, 0, d2, b)
-            w_wait(lsrc, q)
-            if b == -s:
-                w_send(lsrc, q, d2, s)
-    for q, d1, d2, s in each():
-        lsrc = l_at(d1, 2, d2, 0)
-        w_wait(lsrc, q)
-        for step in (1, -1):
-            w_send(lsrc, q, d2, step)
-    x_hop(2)
-    for a in (-1, 1, 2):
+
+    def w_second(a):
         for q, d1, d2, s in each():
             for b in (-s, s):
                 lsrc = l_at(d1, a, d2, b)
                 w_wait(lsrc, q)
                 if b == -s:
                     w_send(lsrc, q, d2, s)
-        if a == 1:
-            x_hop(3)
+
+    x_hop(1, (0, 2))
+    w_first()
+    x_hop(1, (1, 3))
+    w_second(0)
+    x_hop(2, (0, 2))
+    w_long()
+    x_hop(2, (1, 3))
+    w_second(-1)
+    x_hop(3, (0, 2))
+    w_second(1)
+    x_hop(3, (1, 3))
+    w_second(2)
     x_hop(4)
     arrived(xg.at[pl.ds(0, NZ * BLOCKS)], xp_rs)
     for a in (0, -1, 1, 2):
@@ -190,28 +200,31 @@
         at[i] = both.T.astype(bf16)
         return carry
 
-    lax.fori_loop(0, BLOCKS, product, 0)
 
     gathers = (pga, pgb, pg1)
 
     def p_piece(g, vsrc, p):
-        return gathers[g].at[pl.ds(vsrc * BLOCKS + p * 8, 8)]
+        rows = BLOCKS // PIECES
+        return gathers[g].at[pl.ds(vsrc * BLOCKS + p * rows, rows)]
 
     def p_ring(g, vsrc, p, sign, hop):
         ref = p_piece(g, vsrc, p)
         push(ref, ref, p_ss.at[g], p_rs.at[g, 0 if sign > 0 else 1, hop - 1, p], at_z(sign))
 
+    def p_first(g, p):
+        for sign in (1, -1):
+            p_ring(g, v, p, sign, 1)
+        ref = p_piece(g, v, p)
+        push(ref, ref, pp_ss.at[g], pp_rs.at[g], partner)
+
     def p_start(g):
-        for p in range(2):
+        for p in range(PIECES):
+            p_first(g, p)
+
+    def p_hop(g, h):
+        for p in range(PIECES):
             for sign in (1, -1):
-                p_ring(g, v, p, sign, 1)
-        ref = gathers[g].at[pl.ds(v * BLOCKS, BLOCKS)]
-        push(ref, ref, pp_ss.at[g], pp_rs.at[g], partner)
-
-    def p_hop(g, h):
-        for p in range(2):
-            for sign in (1, -1):
-                last = 4 if (p == 0) == (sign > 0) else 3
+                last = 4 if (p % 2 == 0) == (sign > 0) else 3
                 if h > last:
                     continue
                 vsrc = ((z - sign * h + NZ) % NZ) * NC + core
@@ -258,9 +271,11 @@
         j = cand_ref[u - 6, i]
         return jnp.concatenate([pg1[j], xg[j, 1]], axis=0)
 
-    def stage0(u, right):
+    def stage0(u, right, parts=range(4)):
         slot = u % SLOTS
         for q, d1, d2, s in each():
+            if q not in parts:
+                continue
             for i4 in range(4):
                 i = q * 4 + i4
                 term = jnp.dot(at[i], right(u, i), preferred_element_type=f32).astype(bf16)
@@ -338,33 +353,39 @@
         arrived(terms.at[slot, pl.ds(0, 3)], t_ss.at[slot])
         arrived(part.at[slot, pl.ds(0, 3)], r_ss.at[slot])
 
-    p_start(0)
-    stage0(0, right_own)
-    stage0(1, right_own)
+    for q in range(4):
+        lax.fori_loop(q * 4, q * 4 + 4, product, 0, unroll=4)
+        p_first(0, q)
+        stage0(0, right_own, (q,))
+        stage0(1, right_own, (q,))
     p_hop(0, 1)
     stage1(0)
+    p_start(1)
     p_hop(0, 2)
     stage1(1)
+    p_hop(1, 1)
     p_hop(0, 3)
-    p_start(1)
     stage2(0)
+    p_hop(1, 2)
     p_hop(0, 4)
+    p_start(2)
     stage2(1)
+    p_hop(1, 3)
 
     def turn(u, carry):
         def when(low, high, what):
             pl.when((u >= low) & (u < high))(what)
 
-        def hops(*steps):
-            def run():
+        def hops(at, *steps):
+            @pl.when(u == at)
+            def _():
                 for g, h in steps:
                     p_hop(g, h)
                     if (g, h) == (1, 3):
                         p_start(2)
-            return run
-
-        when(4, 5, hops((1, 4)))
-        when(7, 8, hops((2, 4)))
+
+        hops(4, (1, 4))
+        hops(7, (2, 4))
         when(2, 4, lambda: stage0(u, lambda u, i: right_pair(u, i, False)))
         when(4, 6, lambda: stage0(u, lambda u, i: right_pair(u, i, True)))
         when(6, 7, lambda: stage0(u, right_five))
@@ -379,11 +400,9 @@
         when(d + 4, d + 6, lambda: stage4(u - d, "pair"))
         when(d + 6, d + 7, lambda: stage4(u - d, "five"))
         when(d + 7, d + 12, lambda: stage4(u - d, "second"))
-        when(2, 3, hops((1, 1), (1, 2)))
-        when(3, 4, hops((1, 3)))
-        when(4, 5, hops((2, 1)))
-        when(5, 6, hops((2, 2)))
-        when(6, 7, hops((2, 3)))
+        hops(3, (2, 1))
+        hops(4, (2, 2))
+        hops(5, (2, 3))
         return carry
 
     lax.fori_loop(2, CHUNKS + LAGS[3], turn, 0)
@@ -420,7 +439,7 @@
         pltpu.VMEM((CHUNKS, 4, 2, 4, 16, HALF), bf16),
         dma((2, 4, 4)), dma(()), dma(()), dma(()),
         dma((4, 16)), dma(()),
-        dma((3, 2, 4, 2)), dma((3,)), dma((3,)), dma((3,)),
+        dma((3, 2, 4, PIECES)), dma((3,)), dma((3,)), dma((3,)),
         dma((CHUNKS,)), dma((CHUNKS,)), dma((CHUNKS,)), dma((CHUNKS,)), dma((SLOTS,)), dma((SLOTS,)),
     ]
     updated = pl.pallas_call(

time: 163 us -> 149 us (0.914)
  Pallas kernels: 160 us -> 145 us
    pallas_call x1, Pallas kernels: 160 us -> 145 us  [body(): pl.pallas_call(kernel, out_shape=jax.ShapeDtypeStruct((16, 6, BLOCKS, 2 *...]
where the time goes in v3:
time: 149 us; the launch traced here: 148 us
  Pallas kernels  145 us (97%)
  local copies, waits for them, and re-layouts  2.71 us (2%)
    pallas_call x1, Pallas kernels, body(): pl.pallas_call(kernel, out_shape=jax.ShapeDtypeStruct((16, 6, BLOCKS, 2 *...  145 us

profile of v3, /device:TPU:1, one launch (start us, length us, event | category | flops | bytes accessed | tf_op | source)
XLA Modules:
  0.0 147.9 jit_solution(13236703516705752134)
XLA Ops:
  0.0 145.2 %shard_map.55 = f32[16,6,16,256]{3,2,1,0:T(8,128)} custom-call(bf16[64,4096]{1,0:T(8,128)(2,1)} %x_ref.1, f32[16,16,4,256]{3,2,1,0:T(4,128)} %w_ref.1, s32[4,16]{1,0:T(4,128)} %bitcast.5, s32[16]{0:T(128)} %count_ref.1, s32[6,16]{1,0:T(8,128)} %bitcast.4), custom_call_target="tpu_custom_call" | custom-call | tf_op jit(solution)/shard_map/pallas_call | solution.py:445
  145.2 2.7 %copy.7 = f32[16,16,6,256]{3,1,2,0:T(8,128)} copy(f32[16,16,6,256]{3,1,2,0:T(8,128)} %bitcast.3) | data formatting | bytes 3145728

commit v4 on v3

--- a/solution.py
+++ b/solution.py
@@ -33,7 +33,8 @@
     return lax.broadcasted_iota(jnp.int32, shape, len(shape) - 1) < QUARTER
 
 
-def kernel(x_ref, w_ref, pat_ref, count_ref, cand_ref, out_ref,
+def kernel(x_in, w_in, pat_ref, count_ref, cand_ref, out_ref,
+           x_ref, w_ref, in_sem,
            xg, pga, pgb, pg1, own_p, wg, wt, at, hold, terms, fwd1, part, fwd2, m1, m23, n1, n23,
            x_rs, x_ss, xp_rs, xp_ss, w_rs, w_ss, p_rs, p_ss, pp_rs, pp_ss,
            m1_rs, m23_rs, n1_rs, n23_rs, t_ss, r_ss):
@@ -58,6 +59,12 @@
     for device in greeted:
         pl.semaphore_signal(barrier, inc=1, device_id=device, device_id_type=MESH)
 
+    x_copy = pltpu.make_async_copy(x_in, x_ref, in_sem.at[0])
+    w_copy = pltpu.make_async_copy(w_in, w_ref, in_sem.at[1])
+    x_copy.start()
+    w_copy.start()
+
+    x_copy.wait()
     for j in range(BLOCKS):
         for h in range(2):
             start = (j * 2 + h) * HALF
@@ -118,6 +125,7 @@
         for q, (d1, s) in enumerate(PARTS):
             yield q, d1, other(d1), s
 
+    w_copy.wait()
     for q, d1, d2, s in each():
         def load(i4, carry, q=q):
             i = q * 4 + i4
@@ -180,26 +188,32 @@
         for q, d1, d2, s in each():
             w_wait(l_at(d1, a, d2, 2), q)
 
-    def product(i, carry):
-        total = jnp.zeros((SAMP, 2 * HALF), f32)
+    def product(i, half):
+        total = jnp.zeros((SAMP, HALF), f32)
         for k in range(4):
             j = pat_ref[k, i]
             cols = jnp.concatenate([xg[j, 0], xg[j, 1]], axis=1)
-            rows = wg[:, i // 4, i % 4, k].reshape(2 * HALF, 2 * HALF)
+            rows = wg[half * 8:half * 8 + 8, i // 4, i % 4, k].reshape(HALF, 2 * HALF)
             total += lax.dot_general(cols, rows, (((1,), (1,)), ((), ())), preferred_element_type=f32)
-        result = total.astype(bf16)
-        left = total[:, :HALF]
-        other_half = turned(left)
+        return total
+
+    def product_first(i, carry):
+        left = product(i, 0)
+        swapped = turned(left)
         low = low_lanes((SAMP // 2, HALF))
-        pga[v * BLOCKS + i] = jnp.where(low, left[:SAMP // 2], other_half[SAMP // 2:]).astype(bf16)
-        pgb[v * BLOCKS + i] = jnp.where(low, other_half[:SAMP // 2], left[SAMP // 2:]).astype(bf16)
-        own_p[i] = result[:, :HALF]
-        pg1[v * BLOCKS + i] = result[:, HALF:]
-        own = jnp.concatenate([xg[v * BLOCKS + i, 0], xg[v * BLOCKS + i, 1]], axis=1)
-        both = jnp.concatenate([own.astype(f32), result.astype(f32)], axis=0)
-        at[i] = both.T.astype(bf16)
+        pga[v * BLOCKS + i] = jnp.where(low, left[:SAMP // 2], swapped[SAMP // 2:]).astype(bf16)
+        pgb[v * BLOCKS + i] = jnp.where(low, swapped[:SAMP // 2], left[SAMP // 2:]).astype(bf16)
+        own_p[i] = left.astype(bf16)
         return carry
 
+    def product_second(i, carry):
+        result = product(i, 1).astype(bf16)
+        pg1[v * BLOCKS + i] = result
+        both = [jnp.concatenate([xg[v * BLOCKS + i, h].astype(f32), p.astype(f32)], axis=0)
+                for h, p in enumerate((own_p[i], result))]
+        at[i, 0:HALF] = both[0].T.astype(bf16)
+        at[i, HALF:] = both[1].T.astype(bf16)
+        return carry
 
     gathers = (pga, pgb, pg1)
 
@@ -221,8 +235,8 @@
         for p in range(PIECES):
             p_first(g, p)
 
-    def p_hop(g, h):
-        for p in range(PIECES):
+    def p_hop(g, h, pieces=range(PIECES)):
+        for p in pieces:
             for sign in (1, -1):
                 last = 4 if (p % 2 == 0) == (sign > 0) else 3
                 if h > last:
@@ -233,7 +247,7 @@
                 if h < last:
                     p_ring(g, vsrc, p, sign, h + 1)
                 push(ref, ref, pp_ss.at[g], pp_rs.at[g], partner)
-        if h == 4:
+        if h == 4 and PIECES - 1 in pieces:
             arrived(gathers[g].at[pl.ds(0, NZ * BLOCKS)], pp_rs.at[g])
 
     def place(axis, step):
@@ -353,15 +367,25 @@
         arrived(terms.at[slot, pl.ds(0, 3)], t_ss.at[slot])
         arrived(part.at[slot, pl.ds(0, 3)], r_ss.at[slot])
 
-    for q in range(4):
-        lax.fori_loop(q * 4, q * 4 + 4, product, 0, unroll=4)
-        p_first(0, q)
-        stage0(0, right_own, (q,))
-        stage0(1, right_own, (q,))
+    lax.fori_loop(0, 4, product_first, 0, unroll=4)
+    p_first(0, 0)
+    lax.fori_loop(4, 8, product_first, 0, unroll=4)
+    p_first(0, 1)
+    lax.fori_loop(8, 12, product_first, 0, unroll=4)
+    p_first(0, 2)
+    lax.fori_loop(12, 16, product_first, 0, unroll=4)
+    p_first(0, 3)
+    lax.fori_loop(0, 4, product_second, 0, unroll=4)
+    lax.fori_loop(4, 8, product_second, 0, unroll=4)
+    lax.fori_loop(8, 12, product_second, 0, unroll=4)
+    lax.fori_loop(12, 16, product_second, 0, unroll=4)
+    stage0(0, right_own)
     p_hop(0, 1)
+    stage0(1, right_own)
+    p_hop(0, 2, (0, 1))
     stage1(0)
     p_start(1)
-    p_hop(0, 2)
+    p_hop(0, 2, (2, 3))
     stage1(1)
     p_hop(1, 1)
     p_hop(0, 3)
@@ -419,7 +443,11 @@
     vmem = pl.BlockSpec(memory_space=pltpu.VMEM)
     smem = pl.BlockSpec(memory_space=pltpu.SMEM)
     dma = pltpu.SemaphoreType.DMA
+    anywhere = pl.BlockSpec(memory_space=pl.ANY)
     scratch = [
+        pltpu.VMEM(sample_matrix.shape, bf16),
+        pltpu.VMEM(precision_blocks.shape, f32),
+        dma((2,)),
         pltpu.VMEM((256, 2, SAMP, HALF), bf16),
         pltpu.VMEM((256, SAMP // 2, HALF), bf16),
         pltpu.VMEM((256, SAMP // 2, HALF), bf16),
@@ -445,7 +473,7 @@
     updated = pl.pallas_call(
         kernel,
         out_shape=jax.ShapeDtypeStruct((16, 6, BLOCKS, 2 * HALF), f32),
-        in_specs=[vmem, vmem, smem, smem, smem],
+        in_specs=[anywhere, anywhere, smem, smem, smem],
         out_specs=vmem,
         scratch_shapes=scratch,
         compiler_params=pltpu.CompilerParams(

time: 149 us -> 146 us (0.980)
  Pallas kernels: 145 us -> 143 us
    pallas_call x1, Pallas kernels: 145 us -> 143 us  [body(): pl.pallas_call(kernel, out_shape=jax.ShapeDtypeStruct((16, 6, BLOCKS, 2 *...]
where the time goes in v4:
time: 146 us
  Pallas kernels  143 us (98%)
  local copies, waits for them, and re-layouts  2.71 us (2%)
    pallas_call x1, Pallas kernels, body(): pl.pallas_call(kernel, out_shape=jax.ShapeDtypeStruct((16, 6, BLOCKS, 2 *...  143 us

profile of v4, /device:TPU:1, one launch (start us, length us, event | category | flops | bytes accessed | tf_op | source)
XLA Modules:
  0.0 146.1 jit_solution(18148047229159971940)
XLA Ops:
  0.0 143.4 %shard_map.55 = f32[16,6,16,256]{3,2,1,0:T(8,128)} custom-call(bf16[64,4096]{1,0:T(8,128)(2,1)} %x_in.1, f32[16,16,4,256]{3,2,1,0:T(4,128)} %w_in.1, s32[4,16]{1,0:T(4,128)} %bitcast.5, s32[16]{0:T(128)} %count_ref.1, s32[6,16]{1,0:T(8,128)} %bitcast.4), custom_call_target="tpu_custom_call" | custom-call | tf_op jit(solution)/shard_map/pallas_call | solution.py:473
  143.4 2.7 %copy.7 = f32[16,16,6,256]{3,1,2,0:T(8,128)} copy(f32[16,16,6,256]{3,1,2,0:T(8,128)} %bitcast.3) | data formatting | bytes 3145728
